TPU v7x, 32 devices: a whole 2x2x4 slice. The times are simulated.
32 devices in a mesh: batch: 8 (over y, x, core), blk: 4 (over z).
Axes of the slice: x: 2, y: 2, z: 4, core: 2. Of those that a mesh axis runs over, the one named last changes fastest.
Arguments:
- tokens: bfloat16 [16, 1024, 512], P('batch', 'blk'), may hold values from -6 to 6
- lengths: int32 [16], P('batch'), may hold values from 256 to 1024, as said below
- w_query: bfloat16 [512, 512], replicated, may hold values from -0.25 to 0.25
- w_key: bfloat16 [512, 512], replicated, may hold values from -0.25 to 0.25
- w_value: bfloat16 [512, 512], replicated, may hold values from -0.25 to 0.25
- w_out: bfloat16 [512, 512], replicated, may hold values from -1 to 1
- w_in: bfloat16 [512, 2048], replicated, may hold values from -0.25 to 0.25
- b_in: float32 [2048], replicated, may hold values from -3 to 3
- w_back: bfloat16 [2048, 512], replicated, may hold values from -0.125 to 0.125
- b_back: float32 [512], replicated, may hold values from -3 to 3
- alpha_attn: float32 [], replicated, may hold values from 0.3 to 1.2
- alpha_ffn: float32 [], replicated, may hold values from 0.3 to 1.2
- cotangent: bfloat16 [16, 1024, 512], P('batch', 'blk'), may hold values from -6 to 6
Outputs:
- outputs: bfloat16 [16, 1024, 512], P('batch', 'blk')
- grad_input: bfloat16 [16, 1024, 512], P('batch', 'blk')
- grad_w_query: float32 [512, 512], replicated
- grad_w_key: float32 [512, 512], replicated
- grad_w_value: float32 [512, 512], replicated
- grad_w_out: float32 [512, 512], replicated
- grad_w_in: float32 [512, 2048], replicated
- grad_b_in: float32 [2048], replicated
- grad_w_back: float32 [2048, 512], replicated
- grad_b_back: float32 [512], replicated
- grad_alpha_attn: float32 [], replicated
- grad_alpha_ffn: float32 [], replicated
Inputs may be any that keep to these rules, and one draw needn't show every extreme that they name: `lengths`: in each pair of sequences 2i, 2i + 1 one of the two, drawn from the seed, has length 1024; positions at or past a sequence's length are padding.
All inputs are finite; a program needn't handle non-finite values.
Results may differ from a plain program's by a relative error of at most 0.024.
Values may be sent and summed in bfloat16 or wider, within the bound.
A program may use at most 192 MiB of HBM per device.

v0:
```python
import functools

import jax
import jax.numpy as jnp
from jax import lax
from jax.experimental import pallas as pl
from jax.experimental.pallas import tpu as pltpu
from jax.sharding import PartitionSpec as P

HEADS = 8
HEAD_DIM = 64
PAIR = 2 * HEAD_DIM
MESH = pl.DeviceIdType.MESH
BF = jnp.bfloat16
F32 = jnp.float32
NEG = -1e30
GELU_A = 0.7978845608
GELU_B = 0.7978845608 * 0.044715

ORDER = (
    ("start_back", 0), ("block", 0, 0), ("block", 0, 1), ("send", 0, 0), ("attention", 1), ("start_ff", 1),
    ("column", 1, 0), ("sum", 0, 0), ("send", 0, 1), ("sum", 0, 1), ("column", 1, 1),
    ("end_ff", 1), ("small", 0), ("sum", 1, 1), ("sum", 0, 3), ("block", 0, 2), ("sum", 1, 0),
    ("block", 0, 3), ("send", 0, 2), ("sum", 0, 2), ("pass", 0, 0, 0), ("sum", 2, 1), ("end_back", 0),
    ("start_back", 1), ("sum", 1, 3), ("block", 1, 0), ("small", 1), ("sum", 1, 2), ("sum", 3, 1), ("pass", 0, 1, 0),
    ("send", 1, 0), ("pass", 0, 0, 1), ("block", 1, 1), ("sum", 2, 0), ("block", 1, 2), ("small", 2), ("sum", 2, 3),
    ("block", 1, 3), ("small", 3), ("sum", 2, 2), ("sum", 3, 0), ("sum", 3, 2), ("pass", 0, 0, 2), ("sum", 4, 1),
    ("end_back", 1), ("sum", 0, 4), ("sum", 3, 3), ("sum", 0, 5), ("sum", 1, 4), ("sum", 4, 0), ("sum", 1, 5),
    ("sum", 5, 1), ("sum", 4, 2), ("sum", 2, 4), ("send", 1, 2), ("sum", 2, 5), ("pass", 0, 2, 0), ("sum", 6, 1),
    ("sum", 5, 0), ("sum", 5, 2), ("sum", 3, 4), ("sum", 4, 3), ("pass", 0, 1, 1), ("sum", 3, 5), ("sum", 6, 0),
    ("sum", 4, 4), ("sum", 6, 2), ("sum", 5, 3), ("sum", 4, 5), ("sum", 7, 0), ("sum", 5, 4), ("send", 1, 1),
    ("sum", 7, 2), ("pass", 1, 0, 0), ("pass", 1, 0, 2), ("sum", 6, 3), ("sum", 5, 5), ("sum", 6, 4), ("sum", 8, 2),
    ("sum", 6, 5), ("sum", 7, 1), ("pass", 1, 0, 1), ("sum", 8, 0), ("pass", 1, 1, 0), ("sum", 7, 4), ("sum", 8, 1),
    ("sum", 7, 3), ("sum", 7, 5), ("sum", 8, 4), ("sum", 8, 3), ("pass", 1, 2, 0), ("sum", 8, 5), ("pass", 1, 1, 1),
)


class Reducer:
    def __init__(self, nb, nz, rows):
        self.rows, self.nz = rows, nz
        plane = [("batch", 1 << i) for i in range(1, nb.bit_length() - 1)]
        line = [("blk", 1 << i) for i in range(nz.bit_length() - 1)]
        self.all_bits = [("batch", 1)] + plane + line
        direct = (rows // 4 >> len(plane)) // nz >= 16
        steps = line if not direct else [("blk", 0)]
        self.orders = [plane + steps, plane[::-1] + steps]
        self.steps = len(self.orders[0])
        self.kinds, self.sizes, self.lands = [], [], [[], []]
        self.messages = []
        length, land = rows // 4, rows // 2
        for axis, bit in self.orders[0]:
            if bit == 0:
                kind, length, messages = "direct", length // nz, nz - 1
            elif length >= 32:
                kind, length, messages = "half", length // 2, 1
            else:
                kind, messages = "full", 1
            self.kinds.append(kind)
            self.sizes.append(length)
            self.messages.append(messages)
            for o in (0, 1):
                self.lands[o].append(land)
                land += length * messages
        self.land_rows = land
        self.back_steps = [i for i in range(self.steps) if self.kinds[i] != "full"][::-1]
        self.stages = 3 + self.steps + len(self.back_steps)

    def scratch(self, chunks, width):
        return [
            pltpu.VMEM((chunks, self.land_rows, width), BF),
            pltpu.SemaphoreType.DMA((chunks, self.stages - 1)),
            pltpu.SemaphoreType.DMA((chunks, self.stages - 1)),
        ]

    def bind(self, grads, total, land, send_sem, recv_sem):
        self.grads, self.total, self.land = grads, total, land
        self.send_sem, self.recv_sem = send_sem, recv_sem
        self.at = {"batch": lax.axis_index("batch"), "blk": lax.axis_index("blk")}
        core = self.at["batch"] % 2
        half = self.rows // 2
        self.core_keep, self.core_send = core * half, (1 - core) * half
        self.start, self.keep, self.send = [[], []], [[], []], [[], []]
        for o in (0, 1):
            off = self.core_keep + o * (half // 2)
            for i, (axis, bit) in enumerate(self.orders[o]):
                size, here = self.sizes[i], self.at[axis]
                self.start[o].append(off)
                if self.kinds[i] == "half":
                    mine = (here // bit) % 2
                    self.keep[o].append(off + mine * size)
                    self.send[o].append(off + (1 - mine) * size)
                elif self.kinds[i] == "direct":
                    self.keep[o].append(off + here * size)
                    self.send[o].append(None)
                else:
                    self.keep[o].append(off)
                    self.send[o].append(off)
                off = self.keep[o][-1]

    def partner(self, axis, bit):
        mine = (self.at[axis] // bit) % 2
        there = self.at[axis] + bit * (1 - 2 * mine)
        if axis == "batch":
            return (there, self.at["blk"])
        return (self.at["batch"], there)

    def copy(self, c, src, src_row, dst, dst_row, size, sem, device):
        return pltpu.make_async_remote_copy(
            src_ref=src.at[c, pl.ds(pl.multiple_of(src_row, 16), size)],
            dst_ref=dst.at[c, pl.ds(pl.multiple_of(dst_row, 16), size)],
            send_sem=self.send_sem.at[c, sem],
            recv_sem=self.recv_sem.at[c, sem],
            device_id=device,
            device_id_type=MESH,
        )

    def core_out(self, c):
        there = self.partner("batch", 1)
        return self.copy(c, self.grads, self.core_send, self.land, 0, self.rows // 2, 0, there)

    def core_back(self, c):
        there, row, sem = self.partner("batch", 1), self.core_keep, self.stages - 2
        return self.copy(c, self.total, row, self.total, row, self.rows // 2, sem, there)

    def start_out(self, c, i):
        size = self.sizes[i]
        for o in (0, 1):
            axis, bit = self.orders[o][i]
            land = self.lands[o][i]
            if self.kinds[i] != "direct":
                there = self.partner(axis, bit)
                self.copy(c, self.grads, self.send[o][i], self.land, land, size, i + 1, there).start()
                continue
            for d in range(1, self.nz):
                there = (self.at["blk"] + d) % self.nz
                row, peer = self.start[o][i] + there * size, (self.at["batch"], there)
                self.copy(
                    c, self.grads, row, self.land, land + (d - 1) * size, size, i + 1, peer
                ).start()

    def start_back(self, c, place):
        i, sem = self.back_steps[place], self.steps + 1 + place
        for o in (0, 1):
            axis, bit = self.orders[o][i]
            size, row = self.sizes[i], self.keep[o][i]
            peers = [self.partner(axis, bit)]
            if self.kinds[i] == "direct":
                peers = [(self.at["batch"], (self.at["blk"] + d) % self.nz) for d in range(1, self.nz)]
            for peer in peers:
                self.copy(c, self.total, row, self.total, row, size, sem, peer).start()

    def wait(self, c, ref, i, sem):
        rows = 2 * self.sizes[i] * self.messages[i]
        every = self.copy(c, ref, 0, ref, 0, rows, sem, self.partner("batch", 1))
        every.wait_send()
        every.wait_recv()

    def add(self, c, row, land_row, size, pieces=1, last=False):
        part = min(size, 64)
        target = self.total if last else self.grads

        def body(k, carry):
            here = pl.ds(pl.multiple_of(row + k * part, 16), part)
            value = self.grads[c, here]
            if pieces > 1:
                value = value.astype(F32)
            for d in range(pieces):
                there = pl.ds(pl.multiple_of(land_row + d * size + k * part, 16), part)
                value = value + self.land[c, there].astype(value.dtype)
            target[c, here] = value.astype(BF)
            return carry

        lax.fori_loop(0, size // part, body, 0)

    def stage(self, k, c):
        if k == 0:
            self.core_out(c).start()
            return
        if k == 1:
            self.core_out(c).wait()
            self.add(c, self.core_keep, 0, self.rows // 2)
        elif k <= self.steps + 1:
            i = k - 2
            self.wait(c, self.land, i, k - 1)
            pieces = self.nz - 1 if self.kinds[i] == "direct" else 1
            last = i == self.steps - 1
            for o in (0, 1):
                self.add(c, self.keep[o][i], self.lands[o][i], self.sizes[i], pieces, last)
        elif k < self.stages - 1:
            self.wait(c, self.total, self.back_steps[k - self.steps - 2], k - 1)
        else:
            self.core_back(c).wait()
            return
        if k <= self.steps:
            self.start_out(c, k - 1)
        elif k < self.stages - 2:
            self.start_back(c, k - self.steps - 1)
        else:
            self.core_back(c).start()


def mm(left, right):
    return jnp.dot(left, right, preferred_element_type=F32)


def mm_nt(left, right):
    return lax.dot_general(left, right, (((1,), (1,)), ((), ())), preferred_element_type=F32)


def mm_tn(left, right):
    return lax.dot_general(left, right, (((0,), (0,)), ((), ())), preferred_element_type=F32)


def default_order(stages, n, ff_cols, chunks, plane_bits):
    order = [("start_back", 0)] + [("block", 0, j) for j in range(n)] + [("end_back", 0)]
    order += [("attention", 1), ("start_ff", 1)] + [("column", 1, c) for c in range(ff_cols // 2)] + [("end_ff", 1)]
    order += [("start_back", 1)] + [("block", 1, j) for j in range(n)] + [("end_back", 1)]
    order += [("sends", 0), ("sends", 1)]
    order += [("passes", s, hop) for s in (0, 1) for hop in range(n - 1)]
    order += [("small", i) for i in range(plane_bits + 1)]
    for t in range(stages + chunks - 1):
        order += [("sum", k, t - k) for k in range(stages - 1, -1, -1) if 0 <= t - k < chunks]
    return order


def layer_kernel(plan, n, keep, lens, alpha_attn_ref, alpha_ffn_ref, b_in, b_back, *refs):
    (
        tokens_hbm, cot_hbm, wq_hbm, wk_hbm, wv_hbm, wo_hbm, w_in_hbm, w_back_hbm,
        outputs, grad_input, total_out, small_out,
        cot, wq, wk, wv, wo, w_in, w_back, load_sem,
        x_all, wk_t, wv_t, x_t, k_all, v_all, k_t, v_t, q_m, do_m, score, prob_bf, grad_bf, top, norm, o_t, attn_t, do_t,
        live_branch, resid, resid_bf, resid_t, grad_ffn, ffn, grad_x, lse, delta,
        dq_t, dk, dv, acc, back_in,
        x_send, x_recv, r_send, r_recv,
        grads, total, store_sem, land, send_sem, recv_sem, small, small_land, small_line, small_send, small_recv,
    ) = refs
    seqs, _, rows, width = x_all.shape
    chunks = grads.shape[0]
    ff_cols = w_in.shape[1] // width
    pairs = width // PAIR
    plan.bind(grads, total, land, send_sem, recv_sem)
    b, z = lax.axis_index("batch"), lax.axis_index("blk")
    has_up, has_down = z < n - 1, z > 0
    alpha_attn, alpha_ffn = alpha_attn_ref[0], alpha_ffn_ref[0]

    def loop(f, count):
        def body(j, carry):
            f(j)
            return carry

        lax.fori_loop(0, count, body, 0)

    def load(i):
        if i < seqs:
            return pltpu.make_async_copy(tokens_hbm.at[i], x_all.at[i, z], load_sem.at[i])
        pairs_of = [
            (wk_hbm, wk), (wv_hbm, wv), (wq_hbm, wq), (wo_hbm, wo),
            (w_in_hbm, w_in), (w_back_hbm, w_back), (cot_hbm, cot),
        ]
        src, dst = pairs_of[i - seqs]
        return pltpu.make_async_copy(src, dst, load_sem.at[i])

    for i in range(seqs + 7):
        load(i).start()

    def x_copy(s, j, h):
        here = pl.ds(h * (rows // 2), rows // 2)
        return pltpu.make_async_remote_copy(
            src_ref=x_all.at[s, j, here], dst_ref=x_all.at[s, j, here],
            send_sem=x_send.at[s, j, h], recv_sem=x_recv.at[s, j, h],
            device_id=(b, z + 1), device_id_type=MESH,
        )

    def r_copy(s, j, src):
        return pltpu.make_async_remote_copy(
            src_ref=src.at[s, j], dst_ref=back_in.at[s, j],
            send_sem=r_send.at[s, j], recv_sem=r_recv.at[s, j],
            device_id=(b, z - 1), device_id_type=MESH,
        )

    barrier = pltpu.get_barrier_semaphore()
    plane = [(axis, bit) for axis, bit in plan.all_bits if axis == "batch"]
    peers = [plan.partner(axis, bit) for axis, bit in plane] + [(b, (z + d) % n) for d in range(1, n)]
    for peer in peers:
        pl.semaphore_signal(barrier, inc=1, device_id=peer, device_id_type=MESH)
    pl.semaphore_wait(barrier, len(peers))

    def send_own(s):
        @pl.when(has_up)
        def _():
            for h in (0, 1):
                x_copy(s, z, h).start()

    for s in range(seqs):
        load(s).wait()
        if s == 0:
            send_own(0)

    load(seqs).wait()
    wk_t[...] = wk[...].T
    load(seqs + 1).wait()
    wv_t[...] = wv[...].T
    small[0] = jnp.zeros_like(small[0])
    low_lanes = lax.broadcasted_iota(jnp.int32, (rows, PAIR), 1) < HEAD_DIM
    key_iota = lax.broadcasted_iota(jnp.int32, (rows, rows), 0)
    query_pos = z * rows + lax.broadcasted_iota(jnp.int32, (1, rows), 1)

    def split_heads(value, target):
        for h in range(HEADS):
            pair = value[:, (h // 2) * PAIR : (h // 2 + 1) * PAIR]
            mask = low_lanes if h % 2 == 0 else jnp.logical_not(low_lanes)
            target[h // 2, h % 2 * rows : (h % 2 + 1) * rows] = jnp.where(mask, pair, 0.0).astype(BF)

    def slot(s, j):
        return s * n + j if keep else 0

    def forward_slot(s, j):
        return jnp.where((s > 0) & (j == z), n, j) if keep else 0

    def project(s, j):
        here, front = slot(s, j), forward_slot(s, j)
        x = x_all[s, j]
        k_all[front] = mm(x, wk[...]).astype(BF)
        v_all[here] = mm(x, wv[...]).astype(BF)
        k_t[here] = mm_nt(wk_t[...], x).astype(BF)
        v_t[front] = mm_nt(wv_t[...], x).astype(BF)

    def allowed(s, j):
        limit = jnp.minimum(query_pos + 1, lens[s]) - j * rows
        return key_iota < limit

    def scores_of(s, j, head, mask):
        p, half = head // 2, slice(head % 2 * rows, (head % 2 + 1) * rows)
        keys = k_all[forward_slot(s, j), :, p * PAIR : (p + 1) * PAIR]
        return jnp.where(mask, mm_nt(keys, q_m[s, p, half]), NEG)

    def statistics(s, j):
        mask = allowed(s, j)
        for head in range(HEADS):
            score[head] = scores_of(s, j, head, mask)
        for head in range(HEADS):
            old = top[s, head]
            new = jnp.maximum(old, jnp.max(score[head], axis=0, keepdims=True))
            below = jnp.sum(jnp.exp(score[head] - new), axis=0, keepdims=True)
            norm[s, head] = norm[s, head] * jnp.exp(old - new) + below
            top[s, head] = new

    def probabilities(s, j):
        mask = allowed(s, j)
        for head in range(HEADS):
            p, half = head // 2, slice(head % 2 * rows, (head % 2 + 1) * rows)
            probs = jnp.exp(scores_of(s, j, head, mask) - lse[s, head])
            prob_bf[slot(s, j), p, :, half] = probs.astype(BF)

    def mix_values(s, j):
        if not keep:
            project(s, j)
        probabilities(s, j)
        for head in range(HEADS):
            p, half = head // 2, slice(head % 2 * rows, (head % 2 + 1) * rows)
            own = slice(head * HEAD_DIM, (head + 1) * HEAD_DIM)
            o_t[s, own] += mm(v_t[forward_slot(s, j), own], prob_bf[slot(s, j), p, :, half])

    def pass_on(s, j, h):
        x_copy(s, j, h).wait_recv()

        @pl.when(has_up)
        def _():
            x_copy(s, j, h).start()

    def start_seq(s):
        q = mm(x_all[s, z], wq[...]).astype(BF).astype(F32) * 0.125
        split_heads(q, q_m.at[s])
        top[s] = jnp.full_like(top[s], NEG)
        norm[s] = jnp.zeros_like(norm[s])
        o_t[s] = jnp.zeros_like(o_t[s])
        project(s, z)
        statistics(s, z)

    def attention(s):
        def block(i, carry):
            if s == 0:
                for h in (0, 1):
                    pass_on(s, z - i, h)
            else:
                @pl.when((2 * i > ff_cols) | jnp.logical_not(has_up))
                def _():
                    for h in (0, 1):
                        pass_on(s, z - i, h)
            project(s, z - i)
            statistics(s, z - i)
            return carry

        lax.fori_loop(1, z + 1, block, 0)
        if s == 0:
            @pl.when(z > 0)
            def _():
                send_own(1)

            load(seqs + 3).wait()
        lse[s] = top[s] + jnp.log(norm[s])
        loop(functools.partial(mix_values, s), z + 1)
        attn_t[s] = o_t[s].astype(BF)
        branch = mm(attn_t[s].T, wo[...])
        position = z * rows + lax.broadcasted_iota(jnp.int32, (rows, 1), 0)
        live = (position < lens[s]).astype(F32)
        live_branch[s] = live * branch
        resid[...] = x_all[s, z].astype(F32) + alpha_attn * live_branch[s]
        resid_bf[...] = resid[...].astype(BF)
        resid_t[...] = resid_bf[...].T

    def start_feed_forward(s):
        if s == 0:
            for i in (4, 5, 6):
                load(seqs + i).wait()
        grad_out = cot[s].astype(F32)
        grad_ffn[...] = (alpha_ffn * grad_out).astype(BF)
        ffn[...] = jnp.zeros_like(ffn)
        grad_x[s] = grad_out
        small[0, ff_cols : ff_cols + 1] += jnp.sum(
            grad_ffn[...].astype(F32), axis=0, keepdims=True
        )

    def column(s, c):
        lanes = pl.ds(pl.multiple_of(2 * c * width, 2 * width), 2 * width)
        hidden = mm(resid_bf[...], w_in[:, lanes]) + b_in[:, lanes]
        square = hidden * hidden
        half = 0.5 + 0.5 * jnp.tanh(hidden * (GELU_A + GELU_B * square))
        product = hidden * half
        act = product.astype(BF)
        slope = half + product * (1.0 - half) * (2 * GELU_A + 6 * GELU_B * square)
        back = w_back[lanes]
        ffn[...] += mm(act, back)
        grad_hidden = (mm_nt(grad_ffn[...], back) * slope).astype(BF)
        grad_bias = jnp.sum(grad_hidden.astype(F32), axis=0, keepdims=True)
        grad_x[s] += mm_nt(grad_hidden, w_in[:, lanes])
        grad_back = mm(act.T, grad_ffn[...])
        grad_in = mm(resid_t[...], grad_hidden)
        for i in (0, 1):
            chunk, part = 2 * c + i, slice(i * width, (i + 1) * width)
            upper, lower = grad_back[part], grad_in[:, part]
            if s > 0:
                upper += grads[chunk, :width].astype(F32)
                lower += grads[chunk, width:].astype(F32)
            grads[chunk, :width] = upper.astype(BF)
            grads[chunk, width:] = lower.astype(BF)
            small[0, pl.ds(chunk, 1)] += grad_bias[:, part]

    def end_feed_forward(s):
        ffn_out = ffn[...] + b_back[...]
        outputs[s] = (resid[...] + alpha_ffn * ffn_out).astype(BF)
        small[0, ff_cols + 2 : ff_cols + 3] += jnp.sum(
            cot[s].astype(F32) * ffn_out, axis=0, keepdims=True
        )
        small[0, ff_cols + 1 : ff_cols + 2] += jnp.sum(
            grad_x[s] * live_branch[s], axis=0, keepdims=True
        )

    def add_to(k, value, s):
        if s == 0:
            acc[k] = value
        else:
            acc[k] += value

    def start_back(s):
        position = z * rows + lax.broadcasted_iota(jnp.int32, (rows, 1), 0)
        live = (position < lens[s]).astype(F32)
        grad_branch = (alpha_attn * live * grad_x[s]).astype(BF)
        add_to(0, mm(attn_t[s], grad_branch), s)
        do = mm_nt(grad_branch, wo[...]).astype(BF)
        split_heads(do, do_m)
        do_t[...] = mm_nt(wo[...], grad_branch).astype(BF)
        for h in range(HEADS):
            here = slice(h * HEAD_DIM, (h + 1) * HEAD_DIM)
            delta[h] = jnp.sum(do_t[here].astype(F32) * o_t[s, here], axis=0, keepdims=True)
        dq_t[...] = jnp.zeros_like(dq_t)
        if s == 0:
            acc[2] = jnp.zeros_like(acc[2])
            acc[3] = jnp.zeros_like(acc[3])

        @pl.when(has_up)
        def _():
            def sent(j):
                for h in (0, 1):
                    x_copy(s, j, h).wait_send()

            loop(sent, z + 1)

    def block(s, j):
        here = slot(s, j)
        if not keep:
            project(s, j)
            probabilities(s, j)
        for head in range(HEADS):
            p, half = head // 2, slice(head % 2 * rows, (head % 2 + 1) * rows)
            grad_probs = mm_nt(v_all[here, :, p * PAIR : (p + 1) * PAIR], do_m[p, half])
            probs = prob_bf[here, p, :, half].astype(F32)
            grad_bf[p, :, half] = (probs * (grad_probs - delta[head])).astype(BF)
        for p in range(pairs):
            lanes = slice(p * PAIR, (p + 1) * PAIR)
            dv[:, lanes] = mm(prob_bf[here, p], do_m[p]).astype(BF)
            dk[:, lanes] = mm(grad_bf[p], q_m[s, p]).astype(BF)
            for h in (0, 1):
                own = slice(p * PAIR + h * HEAD_DIM, p * PAIR + (h + 1) * HEAD_DIM)
                dq_t[own] += mm(k_t[here, own], grad_bf[p, :, h * rows : (h + 1) * rows])
        part = mm_nt(dk[...], wk[...]) + mm_nt(dv[...], wv[...])
        x_t[...] = x_all[s, j].T
        acc[2] += mm(x_t[...], dk[...])
        acc[3] += mm(x_t[...], dv[...])

        @pl.when(j < z)
        def _():
            x_all[s, j] = part.astype(BF)

        @pl.when(j == z)
        def _():
            grad_x[s] += part

    def send_part(s, j):
        @pl.when(jnp.logical_not(has_up) & (j < z))
        def _():
            r_copy(s, j, x_all).start()

    def end_back(s):
        dq = (dq_t[...] * 0.125).T.astype(BF)
        x_t[...] = x_all[s, z].T
        add_to(1, mm(x_t[...], dq), s)
        grad_x[s] += mm_nt(dq, wq[...])

    def pass_back(s, hop, j):
        @pl.when(z == n - 2 - hop)
        def _():
            r_copy(s, j, back_in).wait_recv()

            @pl.when(j < z)
            def _():
                back_in[s, j] = back_in[s, j] + x_all[s, j]
                r_copy(s, j, back_in).start()

    def finish_input(s):
        @pl.when(has_up)
        def _():
            grad_input[s] = (grad_x[s] + back_in[s, z].astype(F32)).astype(BF)

        @pl.when(jnp.logical_not(has_up))
        def _():
            grad_input[s] = grad_x[s].astype(BF)

    def small_bit(i):
        return pltpu.make_async_remote_copy(
            src_ref=small.at[i], dst_ref=small_land.at[i],
            send_sem=small_send.at[i], recv_sem=small_recv.at[i],
            device_id=plan.partner(*plane[i]), device_id_type=MESH,
        )

    def small_to(d):
        sem = len(plane) + d - 1
        return pltpu.make_async_remote_copy(
            src_ref=small.at[len(plane)], dst_ref=small_line.at[z],
            send_sem=small_send.at[sem], recv_sem=small_recv.at[sem],
            device_id=(b, (z + d) % n), device_id_type=MESH,
        )

    def small_step(i):
        if i > 0:
            small_bit(i - 1).wait()
            small[i] = small[i - 1] + small_land[i - 1]
        if i < len(plane):
            small_bit(i).start()
        else:
            for d in range(1, n):
                small_to(d).start()

    def small_end():
        for d in range(1, n):
            small_to(d).wait()
        small_line[z] = small[len(plane)]
        value = small_line[0]
        for d in range(1, n):
            value = value + small_line[d]
        small_out[...] = value

    def store(c):
        return pltpu.make_async_copy(total.at[c], total_out.at[c], store_sem.at[c])

    def sum_stage(k, c):
        if k == 0 and c >= ff_cols:
            for i in (0, 1):
                part = acc[2 * (c - ff_cols) + i]
                grads[c, i * width : (i + 1) * width] = part.astype(BF)
        plan.stage(k, c)
        if k == plan.stages - 1:
            store(c).start()

    steps = {
        "attention": attention, "start_ff": start_feed_forward, "end_ff": end_feed_forward,
        "start_back": start_back, "block": block, "end_back": end_back, "send": send_part,
        "pass": pass_back, "sum": sum_stage, "small": small_step,
        "sends": lambda s: loop(functools.partial(send_part, s), z),
        "passes": lambda s, hop: loop(functools.partial(pass_back, s, hop), n - 1 - hop),
    }

    load(seqs + 2).wait()
    loop(start_seq, seqs)

    @pl.when(z == 0)
    def _():
        send_own(1)

    attention(0)
    start_feed_forward(0)

    def first_column(c):
        @pl.when((z > c) & has_up)
        def _():
            for h in (0, 1):
                pass_on(1, z - c - 1, h)

        column(0, c)

    loop(first_column, ff_cols // 2)
    end_feed_forward(0)

    if n == 4 and ff_cols == 4 and plan.stages == 9 and seqs == 2:
        order = ORDER
    else:
        order = default_order(plan.stages, n, ff_cols, chunks, len(plane))

    def run(step):
        @pl.when(z >= 0)
        def _():
            steps[step[0]](*step[1:])

    def run_between(group):
        at = [i for i, step in enumerate(group) if step[0] == "column"]
        if not at:
            for step in group:
                run(step)
            return
        for step in group[: at[0]]:
            run(step)

        def one(c):
            column(seqs - 1, c)
            for k in range(ff_cols // 2 - 1):
                inside = group[at[k] + 1 : at[k + 1]]
                if inside:
                    @pl.when(c == k)
                    def _():
                        for step in inside:
                            run(step)

        loop(one, ff_cols // 2)
        for step in group[at[-1] + 1 :]:
            run(step)

    at = [i for i, step in enumerate(order) if step[0] == "block"]
    for step in order[: at[0]]:
        run(step)

    def one_block(t):
        s, j = t // n, t % n

        @pl.when(j <= z)
        def _():
            block(s, j)

        for k in range(len(at) - 1):
            group = order[at[k] + 1 : at[k + 1]]
            if group:
                @pl.when(t == k)
                def _():
                    run_between(group)

    loop(one_block, len(at))
    for step in order[at[-1] + 1 :]:
        run(step)
    for s in range(seqs):
        finish_input(s)
    small_end()
    for c in range(chunks):
        store(c).wait()

    @pl.when(has_down)
    def _():
        for s in range(seqs):
            loop(lambda j: r_copy(s, j, back_in).wait_send(), z)


def expand_kernel(
    cols, total, small, outputs_in, input_in,
    back, w_in, out, query, key, value, outputs, grad_input, b_in, b_back, alpha_attn, alpha_ffn,
    half, full, through, load_sem, store_sem, pass_sem,
):
    chunks, _, width = half.shape
    loads = [pltpu.make_async_copy(total.at[c], half.at[c], load_sem.at[c]) for c in range(chunks)]
    for one in loads:
        one.start()
    arrivals = [
        pltpu.make_async_copy(outputs_in, through.at[0], pass_sem.at[0]),
        pltpu.make_async_copy(input_in, through.at[1], pass_sem.at[1]),
    ]
    for one in arrivals:
        one.start()
    places = []
    for c in range(cols):
        here = pl.ds(c * width, width)
        places.append((back.at[here], w_in.at[:, here]))
    places += [(out, query), (key, value)]
    stores = []
    for c in range(chunks):
        loads[c].wait()
        for i in (0, 1):
            full[c, i] = half[c, i * width : (i + 1) * width].astype(F32)
            stores.append(pltpu.make_async_copy(full.at[c, i], places[c][i], store_sem.at[c, i]))
            stores[-1].start()
    for c in range(cols):
        b_in[:, c * width : (c + 1) * width] = small[c : c + 1]
    b_back[...] = small[cols : cols + 1]
    alpha_attn[...] = jnp.sum(small[cols + 1 : cols + 2], axis=1, keepdims=True)
    alpha_ffn[...] = jnp.sum(small[cols + 2 : cols + 3], axis=1, keepdims=True)
    for i, target in enumerate((outputs, grad_input)):
        arrivals[i].wait()
        stores.append(pltpu.make_async_copy(through.at[i], target, pass_sem.at[2 + i]))
        stores[-1].start()
    for one in stores:
        one.wait()


def expand(total, small, outputs, grad_input, ff):
    chunks, _, width = total.shape
    cols = ff // width
    square = jax.ShapeDtypeStruct((width, width), F32)
    scalar = jax.ShapeDtypeStruct((1, 1), F32)
    vmem = pl.BlockSpec(memory_space=pltpu.VMEM)
    hbm = pl.BlockSpec(memory_space=pl.ANY)
    return pl.pallas_call(
        functools.partial(expand_kernel, cols),
        out_shape=(
            jax.ShapeDtypeStruct((ff, width), F32),
            jax.ShapeDtypeStruct((width, ff), F32),
            square, square, square, square,
            jax.ShapeDtypeStruct(outputs.shape, BF),
            jax.ShapeDtypeStruct(outputs.shape, BF),
            jax.ShapeDtypeStruct((1, ff), F32),
            jax.ShapeDtypeStruct((1, width), F32),
            scalar, scalar,
        ),
        in_specs=[hbm, vmem, hbm, hbm],
        out_specs=(hbm,) * 8 + (vmem,) * 4,
        scratch_shapes=[
            pltpu.VMEM(total.shape, BF),
            pltpu.VMEM((chunks, 2, width, width), F32),
            pltpu.VMEM((2,) + outputs.shape, BF),
            pltpu.SemaphoreType.DMA((chunks,)),
            pltpu.SemaphoreType.DMA((chunks, 2)),
            pltpu.SemaphoreType.DMA((4,)),
        ],
        name="expand",
        compiler_params=pltpu.CompilerParams(vmem_limit_bytes=63 << 20),
    )(total, small, outputs, grad_input)


def per_device(
    tokens, lengths, w_query, w_key, w_value, w_out, w_in, b_in, w_back, b_back,
    alpha_attn, alpha_ffn, cotangent,
):
    seqs, rows, width = tokens.shape
    ff = w_in.shape[1]
    nb, n = lax.axis_size("batch"), lax.axis_size("blk")
    keep = n <= 4
    slots = seqs * n if keep else 1
    ff_cols = ff // width
    chunks = ff_cols + 2
    plan = Reducer(nb, n, 2 * width)
    steps = nb.bit_length() - 1
    small_rows = -(-(ff_cols + 3) // 8) * 8
    vmem = pl.BlockSpec(memory_space=pltpu.VMEM)
    smem = pl.BlockSpec(memory_space=pltpu.SMEM)
    hbm = pl.BlockSpec(memory_space=pl.ANY)
    square = (rows, width)
    dma = pltpu.SemaphoreType.DMA
    outputs, grad_input, total, small = pl.pallas_call(
        functools.partial(layer_kernel, plan, n, keep),
        out_shape=(
            jax.ShapeDtypeStruct(tokens.shape, BF),
            jax.ShapeDtypeStruct(tokens.shape, BF),
            jax.ShapeDtypeStruct((chunks, 2 * width, width), BF),
            jax.ShapeDtypeStruct((small_rows, width), F32),
        ),
        in_specs=[smem] * 3 + [vmem] * 2 + [hbm] * 8,
        out_specs=(vmem, vmem, hbm, vmem),
        scratch_shapes=[
            pltpu.VMEM(tokens.shape, BF),
            pltpu.VMEM((width, width), BF), pltpu.VMEM((width, width), BF),
            pltpu.VMEM((width, width), BF), pltpu.VMEM((width, width), BF),
            pltpu.VMEM(w_in.shape, BF), pltpu.VMEM(w_back.shape, BF),
            dma((seqs + 7,)),
            pltpu.VMEM((seqs, n) + square, BF),
            pltpu.VMEM((width, width), BF),
            pltpu.VMEM((width, width), BF),
            pltpu.VMEM((width, rows), BF),
            pltpu.VMEM((n + 1 if keep else 1,) + square, BF),
            pltpu.VMEM((slots,) + square, BF),
            pltpu.VMEM((slots, width, rows), BF),
            pltpu.VMEM((n + 1 if keep else 1, width, rows), BF),
            pltpu.VMEM((seqs, HEADS // 2, 2 * rows, PAIR), BF),
            pltpu.VMEM((HEADS // 2, 2 * rows, PAIR), BF),
            pltpu.VMEM((HEADS, rows, rows), F32),
            pltpu.VMEM((slots, HEADS // 2, rows, 2 * rows), BF),
            pltpu.VMEM((HEADS // 2, rows, 2 * rows), BF),
            pltpu.VMEM((seqs, HEADS, 1, rows), F32),
            pltpu.VMEM((seqs, HEADS, 1, rows), F32),
            pltpu.VMEM((seqs, width, rows), F32),
            pltpu.VMEM((seqs, width, rows), BF),
            pltpu.VMEM((width, rows), BF),
            pltpu.VMEM((seqs,) + square, F32),
            pltpu.VMEM(square, F32),
            pltpu.VMEM(square, BF),
            pltpu.VMEM((width, rows), BF),
            pltpu.VMEM(square, BF),
            pltpu.VMEM(square, F32),
            pltpu.VMEM((seqs,) + square, F32),
            pltpu.VMEM((seqs, HEADS, 1, rows), F32),
            pltpu.VMEM((HEADS, 1, rows), F32),
            pltpu.VMEM((width, rows), F32),
            pltpu.VMEM(square, BF),
            pltpu.VMEM(square, BF),
            pltpu.VMEM((4, width, width), F32),
            pltpu.VMEM((seqs, n) + square, BF),
            dma((seqs, n, 2)), dma((seqs, n, 2)), dma((seqs, n)), dma((seqs, n)),
            pltpu.VMEM((chunks, 2 * width, width), BF),
            pltpu.VMEM((chunks, 2 * width, width), BF),
            dma((chunks,)),
        ]
        + plan.scratch(chunks, width)
        + [
            pltpu.VMEM((steps + 1, small_rows, width), F32),
            pltpu.VMEM((steps, small_rows, width), F32),
            pltpu.VMEM((n, small_rows, width), F32),
            dma((steps + n - 1,)),
            dma((steps + n - 1,)),
        ],
        name="layer",
        compiler_params=pltpu.CompilerParams(
            collective_id=0, has_side_effects=True, vmem_limit_bytes=63 << 20
        ),
    )(
        lengths, alpha_attn.reshape(1), alpha_ffn.reshape(1), b_in.reshape(1, ff),
        b_back.reshape(1, width), tokens, cotangent, w_query, w_key, w_value, w_out, w_in, w_back,
    )
    back, grad_in, out, query, key, value, outputs, grad_input, b_in, b_back, attn, ffn = expand(
        total, small, outputs, grad_input, ff
    )
    return (
        outputs, grad_input, query, key, value, out, grad_in, b_in.reshape(ff), back,
        b_back.reshape(width), attn.reshape(()), ffn.reshape(()),
    )


def solution(mesh):
    return jax.shard_map(
        per_device,
        mesh=mesh,
        in_specs=(
            P("batch", "blk", None),
            P("batch"),
            P(),
            P(),
            P(),
            P(),
            P(),
            P(),
            P(),
            P(),
            P(),
            P(),
            P("batch", "blk", None),
        ),
        out_specs=(
            P("batch", "blk", None),
            P("batch", "blk", None),
            P(),
            P(),
            P(),
            P(),
            P(),
            P(),
            P(),
            P(),
            P(),
            P(),
        ),
        check_vma=False,
    )
```

profile of v0, /device:TPU:0, one launch (start us, length us, event | category | flops | bytes accessed | tf_op | source)
XLA Modules:
  0.0 127.4 jit_solution(10865218798502233608)
XLA Ops:
  1.9 117.2 %layer.1 = (bf16[2,256,512]{2,1,0:T(8,128)(2,1)}, bf16[2,256,512]{2,1,0:T(8,128)(2,1)}, bf16[6,1024,512]{2,1,0:T(8,128)(2,1)}, f32[8,512]{1,0:T(8,128)}) custom-call(s32[2]{0:T(128)} %lens.1, f32[1]{0:T(128)} %bitcast.8.alpha_attn_ref, f32[1]{0:T(128)} %bitcast.9.alpha_ffn_ref, f32[1,2048]{1,0:T(1,128)} %bitcast.10, f32[1,512]{1,0:T(1,128)} %bitcast.11, ...), custom_call_target="tpu_custom_call" | custom-call | tf_op jit(solution)/shard_map/layer/pallas_call | solution.py:783
  119.1 8.1 %expand.1 = (f32[2048,512]{1,0:T(8,128)}, f32[512,2048]{1,0:T(8,128)}, f32[512,512]{1,0:T(8,128)}, f32[512,512]{1,0:T(8,128)}, f32[512,512]{1,0:T(8,128)}, /*ind...) custom-call(bf16[6,1024,512]{2,1,0:T(8,128)(2,1)} %get-tuple-element, ...), custom_call_target="tpu_custom_call" | custom-call | tf_op jit(solution)/shard_map/expand/pallas_call | solution.py:737
where the time goes:
time: 128 us; the launch traced here: 127 us
  Pallas kernels  125 us (98%)
  between operations  2.11 us (2%)
    pallas_call x1, Pallas kernels, per_device(): pl.pallas_call(functools.partial(layer_kernel, plan, n, keep), out_shape=...  117 us
    pallas_call x1, Pallas kernels, expand(): pl.pallas_call(functools.partial(expand_kernel, cols), out_shape=(jax.Sha...  8.11 us

commit v1 on v0

--- a/solution.py
+++ b/solution.py
@@ -18,20 +18,20 @@
 GELU_B = 0.7978845608 * 0.044715
 
 ORDER = (
-    ("start_back", 0), ("block", 0, 0), ("block", 0, 1), ("send", 0, 0), ("attention", 1), ("start_ff", 1),
-    ("column", 1, 0), ("sum", 0, 0), ("send", 0, 1), ("sum", 0, 1), ("column", 1, 1),
-    ("end_ff", 1), ("small", 0), ("sum", 1, 1), ("sum", 0, 3), ("block", 0, 2), ("sum", 1, 0),
-    ("block", 0, 3), ("send", 0, 2), ("sum", 0, 2), ("pass", 0, 0, 0), ("sum", 2, 1), ("end_back", 0),
-    ("start_back", 1), ("sum", 1, 3), ("block", 1, 0), ("small", 1), ("sum", 1, 2), ("sum", 3, 1), ("pass", 0, 1, 0),
-    ("send", 1, 0), ("pass", 0, 0, 1), ("block", 1, 1), ("sum", 2, 0), ("block", 1, 2), ("small", 2), ("sum", 2, 3),
-    ("block", 1, 3), ("small", 3), ("sum", 2, 2), ("sum", 3, 0), ("sum", 3, 2), ("pass", 0, 0, 2), ("sum", 4, 1),
-    ("end_back", 1), ("sum", 0, 4), ("sum", 3, 3), ("sum", 0, 5), ("sum", 1, 4), ("sum", 4, 0), ("sum", 1, 5),
-    ("sum", 5, 1), ("sum", 4, 2), ("sum", 2, 4), ("send", 1, 2), ("sum", 2, 5), ("pass", 0, 2, 0), ("sum", 6, 1),
-    ("sum", 5, 0), ("sum", 5, 2), ("sum", 3, 4), ("sum", 4, 3), ("pass", 0, 1, 1), ("sum", 3, 5), ("sum", 6, 0),
-    ("sum", 4, 4), ("sum", 6, 2), ("sum", 5, 3), ("sum", 4, 5), ("sum", 7, 0), ("sum", 5, 4), ("send", 1, 1),
-    ("sum", 7, 2), ("pass", 1, 0, 0), ("pass", 1, 0, 2), ("sum", 6, 3), ("sum", 5, 5), ("sum", 6, 4), ("sum", 8, 2),
-    ("sum", 6, 5), ("sum", 7, 1), ("pass", 1, 0, 1), ("sum", 8, 0), ("pass", 1, 1, 0), ("sum", 7, 4), ("sum", 8, 1),
-    ("sum", 7, 3), ("sum", 7, 5), ("sum", 8, 4), ("sum", 8, 3), ("pass", 1, 2, 0), ("sum", 8, 5), ("pass", 1, 1, 1),
+    ("start_back", 0), ("block", 0, 0), ("send", 0, 0), ("block", 0, 1), ("send", 0, 1), ("attention", 1),
+    ("start_ff", 1), ("column", 1, 0), ("sum", 0, 1), ("column", 1, 1), ("sum", 0, 0), ("sum", 0, 2), ("sum", 0, 3),
+    ("sum", 1, 1), ("pass", 0, 0, 0), ("pass", 0, 0, 1), ("end_ff", 1), ("small", 0), ("block", 0, 2),
+    ("block", 0, 3), ("send", 0, 2), ("sum", 1, 0), ("end_back", 0), ("sum", 1, 2), ("start_back", 1),
+    ("block", 1, 0), ("small", 1), ("block", 1, 1), ("send", 1, 1), ("sum", 2, 0), ("block", 1, 2), ("small", 2),
+    ("pass", 0, 1, 0), ("sum", 2, 1), ("sum", 2, 2), ("block", 1, 3), ("small", 3), ("sum", 3, 0), ("end_back", 1),
+    ("sum", 0, 4), ("sum", 1, 3), ("sum", 3, 1), ("sum", 3, 2), ("sum", 1, 4), ("sum", 0, 5), ("sum", 1, 5),
+    ("sum", 4, 0), ("sum", 2, 4), ("sum", 4, 2), ("sum", 2, 5), ("sum", 2, 3), ("sum", 4, 1), ("sum", 3, 5),
+    ("sum", 5, 2), ("sum", 3, 4), ("sum", 5, 0), ("sum", 5, 1), ("sum", 6, 2), ("sum", 3, 3), ("sum", 6, 0),
+    ("sum", 4, 5), ("sum", 4, 4), ("send", 1, 0), ("sum", 4, 3), ("sum", 6, 1), ("sum", 5, 5), ("sum", 7, 2),
+    ("sum", 5, 4), ("send", 1, 2), ("sum", 6, 5), ("pass", 1, 0, 0), ("sum", 5, 3), ("sum", 6, 4), ("pass", 0, 1, 1),
+    ("sum", 7, 5), ("pass", 1, 0, 1), ("pass", 0, 0, 2), ("sum", 6, 3), ("pass", 1, 1, 0), ("sum", 7, 1),
+    ("sum", 7, 0), ("sum", 8, 5), ("sum", 7, 4), ("sum", 7, 3), ("pass", 1, 0, 2), ("pass", 1, 1, 1), ("sum", 8, 4),
+    ("sum", 8, 2), ("pass", 0, 2, 0), ("sum", 8, 0), ("pass", 1, 2, 0), ("sum", 8, 1), ("sum", 8, 3),
 )
 
 
@@ -226,13 +226,13 @@
 def layer_kernel(plan, n, keep, lens, alpha_attn_ref, alpha_ffn_ref, b_in, b_back, *refs):
     (
         tokens_hbm, cot_hbm, wq_hbm, wk_hbm, wv_hbm, wo_hbm, w_in_hbm, w_back_hbm,
-        outputs, grad_input, total_out, small_out,
+        outputs, grad_input, total, small_out,
         cot, wq, wk, wv, wo, w_in, w_back, load_sem,
         x_all, wk_t, wv_t, x_t, k_all, v_all, k_t, v_t, q_m, do_m, score, prob_bf, grad_bf, top, norm, o_t, attn_t, do_t,
         live_branch, resid, resid_bf, resid_t, grad_ffn, ffn, grad_x, lse, delta,
         dq_t, dk, dv, acc, back_in,
         x_send, x_recv, r_send, r_recv,
-        grads, total, store_sem, land, send_sem, recv_sem, small, small_land, small_line, small_send, small_recv,
+        grads, land, send_sem, recv_sem, small, small_land, small_line, small_send, small_recv,
     ) = refs
     seqs, _, rows, width = x_all.shape
     chunks = grads.shape[0]
@@ -580,17 +580,12 @@
             value = value + small_line[d]
         small_out[...] = value
 
-    def store(c):
-        return pltpu.make_async_copy(total.at[c], total_out.at[c], store_sem.at[c])
-
     def sum_stage(k, c):
         if k == 0 and c >= ff_cols:
             for i in (0, 1):
                 part = acc[2 * (c - ff_cols) + i]
                 grads[c, i * width : (i + 1) * width] = part.astype(BF)
         plan.stage(k, c)
-        if k == plan.stages - 1:
-            store(c).start()
 
     steps = {
         "attention": attention, "start_ff": start_feed_forward, "end_ff": end_feed_forward,
@@ -678,9 +673,6 @@
     for s in range(seqs):
         finish_input(s)
     small_end()
-    for c in range(chunks):
-        store(c).wait()
-
     @pl.when(has_down)
     def _():
         for s in range(seqs):
@@ -690,28 +682,23 @@
 def expand_kernel(
     cols, total, small, outputs_in, input_in,
     back, w_in, out, query, key, value, outputs, grad_input, b_in, b_back, alpha_attn, alpha_ffn,
-    half, full, through, load_sem, store_sem, pass_sem,
+    full, store_sem, pass_sem,
 ):
-    chunks, _, width = half.shape
-    loads = [pltpu.make_async_copy(total.at[c], half.at[c], load_sem.at[c]) for c in range(chunks)]
-    for one in loads:
-        one.start()
-    arrivals = [
-        pltpu.make_async_copy(outputs_in, through.at[0], pass_sem.at[0]),
-        pltpu.make_async_copy(input_in, through.at[1], pass_sem.at[1]),
+    chunks, _, width = total.shape
+    stores = [
+        pltpu.make_async_copy(outputs_in, outputs, pass_sem.at[0]),
+        pltpu.make_async_copy(input_in, grad_input, pass_sem.at[1]),
     ]
-    for one in arrivals:
+    for one in stores:
         one.start()
     places = []
     for c in range(cols):
         here = pl.ds(c * width, width)
         places.append((back.at[here], w_in.at[:, here]))
     places += [(out, query), (key, value)]
-    stores = []
     for c in range(chunks):
-        loads[c].wait()
         for i in (0, 1):
-            full[c, i] = half[c, i * width : (i + 1) * width].astype(F32)
+            full[c, i] = total[c, i * width : (i + 1) * width].astype(F32)
             stores.append(pltpu.make_async_copy(full.at[c, i], places[c][i], store_sem.at[c, i]))
             stores[-1].start()
     for c in range(cols):
@@ -719,10 +706,6 @@
     b_back[...] = small[cols : cols + 1]
     alpha_attn[...] = jnp.sum(small[cols + 1 : cols + 2], axis=1, keepdims=True)
     alpha_ffn[...] = jnp.sum(small[cols + 2 : cols + 3], axis=1, keepdims=True)
-    for i, target in enumerate((outputs, grad_input)):
-        arrivals[i].wait()
-        stores.append(pltpu.make_async_copy(through.at[i], target, pass_sem.at[2 + i]))
-        stores[-1].start()
     for one in stores:
         one.wait()
 
@@ -746,18 +729,15 @@
             jax.ShapeDtypeStruct((1, width), F32),
             scalar, scalar,
         ),
-        in_specs=[hbm, vmem, hbm, hbm],
+        in_specs=[vmem] * 4,
         out_specs=(hbm,) * 8 + (vmem,) * 4,
         scratch_shapes=[
-            pltpu.VMEM(total.shape, BF),
             pltpu.VMEM((chunks, 2, width, width), F32),
-            pltpu.VMEM((2,) + outputs.shape, BF),
-            pltpu.SemaphoreType.DMA((chunks,)),
             pltpu.SemaphoreType.DMA((chunks, 2)),
-            pltpu.SemaphoreType.DMA((4,)),
+            pltpu.SemaphoreType.DMA((2,)),
         ],
         name="expand",
-        compiler_params=pltpu.CompilerParams(vmem_limit_bytes=63 << 20),
+        compiler_params=pltpu.CompilerParams(vmem_limit_bytes=40 << 20),
     )(total, small, outputs, grad_input)
 
 
@@ -783,13 +763,13 @@
     outputs, grad_input, total, small = pl.pallas_call(
         functools.partial(layer_kernel, plan, n, keep),
         out_shape=(
-            jax.ShapeDtypeStruct(tokens.shape, BF),
-            jax.ShapeDtypeStruct(tokens.shape, BF),
-            jax.ShapeDtypeStruct((chunks, 2 * width, width), BF),
-            jax.ShapeDtypeStruct((small_rows, width), F32),
+            pltpu.VMEM(tokens.shape, BF),
+            pltpu.VMEM(tokens.shape, BF),
+            pltpu.VMEM((chunks, 2 * width, width), BF),
+            pltpu.VMEM((small_rows, width), F32),
         ),
         in_specs=[smem] * 3 + [vmem] * 2 + [hbm] * 8,
-        out_specs=(vmem, vmem, hbm, vmem),
+        out_specs=(vmem,) * 4,
         scratch_shapes=[
             pltpu.VMEM(tokens.shape, BF),
             pltpu.VMEM((width, width), BF), pltpu.VMEM((width, width), BF),
@@ -830,8 +810,6 @@
             pltpu.VMEM((seqs, n) + square, BF),
             dma((seqs, n, 2)), dma((seqs, n, 2)), dma((seqs, n)), dma((seqs, n)),
             pltpu.VMEM((chunks, 2 * width, width), BF),
-            pltpu.VMEM((chunks, 2 * width, width), BF),
-            dma((chunks,)),
         ]
         + plan.scratch(chunks, width)
         + [
@@ -843,7 +821,7 @@
         ],
         name="layer",
         compiler_params=pltpu.CompilerParams(
-            collective_id=0, has_side_effects=True, vmem_limit_bytes=63 << 20
+            collective_id=0, has_side_effects=True, vmem_limit_bytes=113 << 19
         ),
     )(
         lengths, alpha_attn.reshape(1), alpha_ffn.reshape(1), b_in.reshape(1, ff),

time: 128 us -> 123 us (0.961)
  Pallas kernels: 125 us -> 121 us
    pallas_call x1, Pallas kernels: 8.11 us -> 5.67 us  [expand(): pl.pallas_call(functools.partial(expand_kernel, cols), out_shape=(jax.Sha...]
    pallas_call x1, Pallas kernels: 117 us -> 115 us  [per_device(): pl.pallas_call(functools.partial(layer_kernel, plan, n, keep), out_shape=...]
where the time goes in v1:
time: 123 us
  Pallas kernels  121 us (98%)
  between operations  2.11 us (2%)
    pallas_call x1, Pallas kernels, per_device(): pl.pallas_call(functools.partial(layer_kernel, plan, n, keep), out_shape=...  115 us
    pallas_call x1, Pallas kernels, expand(): pl.pallas_call(functools.partial(expand_kernel, cols), out_shape=(jax.Sha...  5.67 us

profile of v1, /device:TPU:0, one launch (start us, length us, event | category | flops | bytes accessed | tf_op | source)
XLA Modules:
  0.0 123.1 jit_solution(16685902627949826279)
XLA Ops:
  1.9 115.3 %layer.1 = (bf16[2,256,512]{2,1,0:T(8,128)(2,1)S(1)}, bf16[2,256,512]{2,1,0:T(8,128)(2,1)S(1)}, bf16[6,1024,512]{2,1,0:T(8,128)(2,1)S(1)}, f32[8,512]{1,0:T(8,128)S(1)}) custom-call(s32[2]{0:T(128)} %lens.1, f32[1]{0:T(128)} %bitcast.8.alpha_attn_ref, f32[1]{0:T(128)} %bitcast.9.alpha_ffn_ref, f32[1,2048]{1,0:T(1,128)} %bitcast.10, f32[1,512]{1,0:T(1,128)} %bitcast.11, ...), custom_call_target="tpu_custom_call" | custom-call | tf_op jit(solution)/shard_map/layer/pallas_call | solution.py:763
  117.3 5.7 %expand.1 = (f32[2048,512]{1,0:T(8,128)}, f32[512,2048]{1,0:T(8,128)}, f32[512,512]{1,0:T(8,128)}, f32[512,512]{1,0:T(8,128)}, f32[512,512]{1,0:T(8,128)}, /*ind...) custom-call(bf16[6,1024,512]{2,1,0:T(8,128)(2,1)S(1)} %get-tuple-ele, ...), custom_call_target="tpu_custom_call" | custom-call | tf_op jit(solution)/shard_map/expand/pallas_call | solution.py:720

commit v2 on v1

--- a/solution.py
+++ b/solution.py
@@ -18,20 +18,20 @@
 GELU_B = 0.7978845608 * 0.044715
 
 ORDER = (
-    ("start_back", 0), ("block", 0, 0), ("send", 0, 0), ("block", 0, 1), ("send", 0, 1), ("attention", 1),
-    ("start_ff", 1), ("column", 1, 0), ("sum", 0, 1), ("column", 1, 1), ("sum", 0, 0), ("sum", 0, 2), ("sum", 0, 3),
-    ("sum", 1, 1), ("pass", 0, 0, 0), ("pass", 0, 0, 1), ("end_ff", 1), ("small", 0), ("block", 0, 2),
-    ("block", 0, 3), ("send", 0, 2), ("sum", 1, 0), ("end_back", 0), ("sum", 1, 2), ("start_back", 1),
-    ("block", 1, 0), ("small", 1), ("block", 1, 1), ("send", 1, 1), ("sum", 2, 0), ("block", 1, 2), ("small", 2),
-    ("pass", 0, 1, 0), ("sum", 2, 1), ("sum", 2, 2), ("block", 1, 3), ("small", 3), ("sum", 3, 0), ("end_back", 1),
-    ("sum", 0, 4), ("sum", 1, 3), ("sum", 3, 1), ("sum", 3, 2), ("sum", 1, 4), ("sum", 0, 5), ("sum", 1, 5),
-    ("sum", 4, 0), ("sum", 2, 4), ("sum", 4, 2), ("sum", 2, 5), ("sum", 2, 3), ("sum", 4, 1), ("sum", 3, 5),
-    ("sum", 5, 2), ("sum", 3, 4), ("sum", 5, 0), ("sum", 5, 1), ("sum", 6, 2), ("sum", 3, 3), ("sum", 6, 0),
-    ("sum", 4, 5), ("sum", 4, 4), ("send", 1, 0), ("sum", 4, 3), ("sum", 6, 1), ("sum", 5, 5), ("sum", 7, 2),
-    ("sum", 5, 4), ("send", 1, 2), ("sum", 6, 5), ("pass", 1, 0, 0), ("sum", 5, 3), ("sum", 6, 4), ("pass", 0, 1, 1),
-    ("sum", 7, 5), ("pass", 1, 0, 1), ("pass", 0, 0, 2), ("sum", 6, 3), ("pass", 1, 1, 0), ("sum", 7, 1),
-    ("sum", 7, 0), ("sum", 8, 5), ("sum", 7, 4), ("sum", 7, 3), ("pass", 1, 0, 2), ("pass", 1, 1, 1), ("sum", 8, 4),
-    ("sum", 8, 2), ("pass", 0, 2, 0), ("sum", 8, 0), ("pass", 1, 2, 0), ("sum", 8, 1), ("sum", 8, 3),
+    ("start_back", 0), ("block", 0, 0), ("block", 0, 1), ("send", 0, 0), ("attention", 1), ("start_ff", 1),
+    ("column", 1, 0), ("sum", 0, 0), ("send", 0, 1), ("column", 1, 1), ("sum", 0, 2), ("end_ff", 1), ("small", 0),
+    ("sum", 1, 0), ("sum", 0, 1), ("pass", 0, 0, 0), ("block", 0, 2), ("sum", 1, 2), ("send", 0, 2), ("sum", 0, 3),
+    ("block", 0, 3), ("sum", 2, 0), ("end_back", 0), ("pass", 0, 1, 0), ("sum", 1, 3), ("start_back", 1),
+    ("block", 1, 0), ("small", 1), ("sum", 3, 0), ("pass", 0, 0, 1), ("sum", 2, 2), ("block", 1, 1), ("send", 1, 1),
+    ("sum", 1, 1), ("block", 1, 2), ("small", 2), ("block", 1, 3), ("small", 3), ("end_back", 1), ("pass", 0, 0, 2),
+    ("pass", 0, 1, 1), ("sum", 0, 4), ("sum", 2, 3), ("sum", 2, 1), ("sum", 0, 5), ("sum", 3, 2), ("sum", 4, 0),
+    ("sum", 1, 4), ("sum", 1, 5), ("sum", 3, 1), ("sum", 3, 3), ("sum", 4, 2), ("sum", 2, 4), ("sum", 5, 0),
+    ("sum", 4, 1), ("sum", 2, 5), ("sum", 3, 4), ("sum", 5, 2), ("sum", 3, 5), ("sum", 6, 0), ("sum", 5, 1),
+    ("sum", 4, 3), ("sum", 6, 2), ("send", 1, 0), ("sum", 6, 1), ("sum", 4, 5), ("sum", 4, 4), ("sum", 5, 3),
+    ("send", 1, 2), ("pass", 1, 0, 0), ("sum", 7, 1), ("sum", 6, 3), ("sum", 5, 5), ("pass", 1, 0, 1), ("sum", 5, 4),
+    ("sum", 6, 5), ("pass", 1, 1, 0), ("sum", 6, 4), ("sum", 7, 3), ("sum", 7, 2), ("sum", 7, 0), ("pass", 0, 2, 0),
+    ("sum", 7, 5), ("sum", 8, 1), ("sum", 7, 4), ("pass", 1, 2, 0), ("sum", 8, 3), ("sum", 8, 2), ("sum", 8, 0),
+    ("pass", 1, 0, 2), ("sum", 8, 4), ("pass", 1, 1, 1), ("sum", 8, 5),
 )
 
 
@@ -223,12 +223,12 @@
     return order
 
 
-def layer_kernel(plan, n, keep, lens, alpha_attn_ref, alpha_ffn_ref, b_in, b_back, *refs):
+def layer_kernel(plan, n, keep, lens, alpha_attn_ref, alpha_ffn_ref, *refs):
     (
-        tokens_hbm, cot_hbm, wq_hbm, wk_hbm, wv_hbm, wo_hbm, w_in_hbm, w_back_hbm,
+        b_in_hbm, b_back_hbm, tokens_hbm, cot_hbm, wq_hbm, wk_hbm, wv_hbm, wo_hbm, w_in_hbm, w_back_hbm,
         outputs, grad_input, total, small_out,
-        cot, wq, wk, wv, wo, w_in, w_back, load_sem,
-        x_all, wk_t, wv_t, x_t, k_all, v_all, k_t, v_t, q_m, do_m, score, prob_bf, grad_bf, top, norm, o_t, attn_t, do_t,
+        b_in, b_back, cot, wq, wk, wv, wo, w_in, w_back, load_sem,
+        x_all, x_t, k_all, v_all, k_t, v_t, q_m, do_m, score, prob_bf, grad_bf, top, norm, o_t, attn_t, do_t,
         live_branch, resid, resid_bf, resid_t, grad_ffn, ffn, grad_x, lse, delta,
         dq_t, dk, dv, acc, back_in,
         x_send, x_recv, r_send, r_recv,
@@ -255,12 +255,12 @@
             return pltpu.make_async_copy(tokens_hbm.at[i], x_all.at[i, z], load_sem.at[i])
         pairs_of = [
             (wk_hbm, wk), (wv_hbm, wv), (wq_hbm, wq), (wo_hbm, wo),
-            (w_in_hbm, w_in), (w_back_hbm, w_back), (cot_hbm, cot),
+            (w_in_hbm, w_in), (w_back_hbm, w_back), (cot_hbm, cot), (b_in_hbm, b_in), (b_back_hbm, b_back),
         ]
         src, dst = pairs_of[i - seqs]
         return pltpu.make_async_copy(src, dst, load_sem.at[i])
 
-    for i in range(seqs + 7):
+    for i in range(seqs + 9):
         load(i).start()
 
     def x_copy(s, j, h):
@@ -296,10 +296,8 @@
         if s == 0:
             send_own(0)
 
-    load(seqs).wait()
-    wk_t[...] = wk[...].T
-    load(seqs + 1).wait()
-    wv_t[...] = wv[...].T
+    for i in range(3):
+        load(seqs + i).wait()
     small[0] = jnp.zeros_like(small[0])
     low_lanes = lax.broadcasted_iota(jnp.int32, (rows, PAIR), 1) < HEAD_DIM
     key_iota = lax.broadcasted_iota(jnp.int32, (rows, rows), 0)
@@ -320,10 +318,9 @@
     def project(s, j):
         here, front = slot(s, j), forward_slot(s, j)
         x = x_all[s, j]
-        k_all[front] = mm(x, wk[...]).astype(BF)
-        v_all[here] = mm(x, wv[...]).astype(BF)
-        k_t[here] = mm_nt(wk_t[...], x).astype(BF)
-        v_t[front] = mm_nt(wv_t[...], x).astype(BF)
+        keys, values = mm(x, wk[...]).astype(BF), mm(x, wv[...]).astype(BF)
+        k_all[front], v_all[here] = keys, values
+        k_t[here], v_t[front] = keys.T, values.T
 
     def allowed(s, j):
         limit = jnp.minimum(query_pos + 1, lens[s]) - j * rows
@@ -411,7 +408,7 @@
 
     def start_feed_forward(s):
         if s == 0:
-            for i in (4, 5, 6):
+            for i in range(4, 9):
                 load(seqs + i).wait()
         grad_out = cot[s].astype(F32)
         grad_ffn[...] = (alpha_ffn * grad_out).astype(BF)
@@ -595,7 +592,6 @@
         "passes": lambda s, hop: loop(functools.partial(pass_back, s, hop), n - 1 - hop),
     }
 
-    load(seqs + 2).wait()
     loop(start_seq, seqs)
 
     @pl.when(z == 0)
@@ -768,17 +764,16 @@
             pltpu.VMEM((chunks, 2 * width, width), BF),
             pltpu.VMEM((small_rows, width), F32),
         ),
-        in_specs=[smem] * 3 + [vmem] * 2 + [hbm] * 8,
+        in_specs=[smem] * 3 + [hbm] * 10,
         out_specs=(vmem,) * 4,
         scratch_shapes=[
+            pltpu.VMEM((1, ff), F32), pltpu.VMEM((1, width), F32),
             pltpu.VMEM(tokens.shape, BF),
             pltpu.VMEM((width, width), BF), pltpu.VMEM((width, width), BF),
             pltpu.VMEM((width, width), BF), pltpu.VMEM((width, width), BF),
             pltpu.VMEM(w_in.shape, BF), pltpu.VMEM(w_back.shape, BF),
-            dma((seqs + 7,)),
+            dma((seqs + 9,)),
             pltpu.VMEM((seqs, n) + square, BF),
-            pltpu.VMEM((width, width), BF),
-            pltpu.VMEM((width, width), BF),
             pltpu.VMEM((width, rows), BF),
             pltpu.VMEM((n + 1 if keep else 1,) + square, BF),
             pltpu.VMEM((slots,) + square, BF),

time: 123 us -> 120 us (0.976)
  Pallas kernels: 121 us -> 118 us
    pallas_call x1, Pallas kernels: 115 us -> 112 us  [per_device(): pl.pallas_call(functools.partial(layer_kernel, plan, n, keep), out_shape=...]
where the time goes in v2:
time: 120 us
  Pallas kernels  118 us (98%)
  between operations  2.11 us (2%)
    pallas_call x1, Pallas kernels, per_device(): pl.pallas_call(functools.partial(layer_kernel, plan, n, keep), out_shape=...  112 us
    pallas_call x1, Pallas kernels, expand(): pl.pallas_call(functools.partial(expand_kernel, cols), out_shape=(jax.Sha...  5.67 us

profile of v2, /device:TPU:0, one launch (start us, length us, event | category | flops | bytes accessed | tf_op | source)
XLA Modules:
  0.0 120.2 jit_solution(14739002977315345848)
XLA Ops:
  1.9 112.4 %layer.1 = (bf16[2,256,512]{2,1,0:T(8,128)(2,1)S(1)}, bf16[2,256,512]{2,1,0:T(8,128)(2,1)S(1)}, bf16[6,1024,512]{2,1,0:T(8,128)(2,1)S(1)}, f32[8,512]{1,0:T(8,128)S(1)}) custom-call(s32[2]{0:T(128)} %lens.1, f32[1]{0:T(128)} %bitcast.8.alpha_attn_ref, f32[1]{0:T(128)} %bitcast.9.alpha_ffn_ref, f32[1,2048]{1,0:T(1,128)} %bitcast.10, f32[1,512]{1,0:T(1,128)} %bitcast.11, ...), custom_call_target="tpu_custom_call" | custom-call | tf_op jit(solution)/shard_map/layer/pallas_call | solution.py:759
  114.4 5.7 %expand.1 = (f32[2048,512]{1,0:T(8,128)}, f32[512,2048]{1,0:T(8,128)}, f32[512,512]{1,0:T(8,128)}, f32[512,512]{1,0:T(8,128)}, f32[512,512]{1,0:T(8,128)}, /*ind...) custom-call(bf16[6,1024,512]{2,1,0:T(8,128)(2,1)S(1)} %get-tuple-ele, ...), custom_call_target="tpu_custom_call" | custom-call | tf_op jit(solution)/shard_map/expand/pallas_call | solution.py:716

commit v3 on v2

--- a/solution.py
+++ b/solution.py
@@ -18,20 +18,20 @@
 GELU_B = 0.7978845608 * 0.044715
 
 ORDER = (
-    ("start_back", 0), ("block", 0, 0), ("block", 0, 1), ("send", 0, 0), ("attention", 1), ("start_ff", 1),
-    ("column", 1, 0), ("sum", 0, 0), ("send", 0, 1), ("column", 1, 1), ("sum", 0, 2), ("end_ff", 1), ("small", 0),
-    ("sum", 1, 0), ("sum", 0, 1), ("pass", 0, 0, 0), ("block", 0, 2), ("sum", 1, 2), ("send", 0, 2), ("sum", 0, 3),
-    ("block", 0, 3), ("sum", 2, 0), ("end_back", 0), ("pass", 0, 1, 0), ("sum", 1, 3), ("start_back", 1),
-    ("block", 1, 0), ("small", 1), ("sum", 3, 0), ("pass", 0, 0, 1), ("sum", 2, 2), ("block", 1, 1), ("send", 1, 1),
-    ("sum", 1, 1), ("block", 1, 2), ("small", 2), ("block", 1, 3), ("small", 3), ("end_back", 1), ("pass", 0, 0, 2),
-    ("pass", 0, 1, 1), ("sum", 0, 4), ("sum", 2, 3), ("sum", 2, 1), ("sum", 0, 5), ("sum", 3, 2), ("sum", 4, 0),
-    ("sum", 1, 4), ("sum", 1, 5), ("sum", 3, 1), ("sum", 3, 3), ("sum", 4, 2), ("sum", 2, 4), ("sum", 5, 0),
-    ("sum", 4, 1), ("sum", 2, 5), ("sum", 3, 4), ("sum", 5, 2), ("sum", 3, 5), ("sum", 6, 0), ("sum", 5, 1),
-    ("sum", 4, 3), ("sum", 6, 2), ("send", 1, 0), ("sum", 6, 1), ("sum", 4, 5), ("sum", 4, 4), ("sum", 5, 3),
-    ("send", 1, 2), ("pass", 1, 0, 0), ("sum", 7, 1), ("sum", 6, 3), ("sum", 5, 5), ("pass", 1, 0, 1), ("sum", 5, 4),
-    ("sum", 6, 5), ("pass", 1, 1, 0), ("sum", 6, 4), ("sum", 7, 3), ("sum", 7, 2), ("sum", 7, 0), ("pass", 0, 2, 0),
-    ("sum", 7, 5), ("sum", 8, 1), ("sum", 7, 4), ("pass", 1, 2, 0), ("sum", 8, 3), ("sum", 8, 2), ("sum", 8, 0),
-    ("pass", 1, 0, 2), ("sum", 8, 4), ("pass", 1, 1, 1), ("sum", 8, 5),
+    ("start_back", 0), ("block", 0, 0), ("block", 0, 1), ("send", 0, 0), ("send", 0, 1), ("attention", 1),
+    ("start_ff", 1), ("column", 1, 0), ("sum", 0, 0), ("column", 1, 1), ("end_ff", 1), ("small", 0),
+    ("pass", 0, 0, 0), ("sum", 0, 3), ("sum", 1, 0), ("sum", 0, 1), ("block", 0, 2), ("sum", 1, 3), ("send", 0, 2),
+    ("block", 0, 3), ("end_back", 0), ("sum", 0, 2), ("sum", 2, 0), ("pass", 0, 0, 1), ("sum", 1, 1),
+    ("start_back", 1), ("block", 1, 0), ("small", 1), ("sum", 2, 3), ("sum", 1, 2), ("sum", 3, 0), ("block", 1, 1),
+    ("block", 1, 2), ("small", 2), ("pass", 0, 1, 0), ("pass", 0, 2, 0), ("sum", 2, 1), ("sum", 3, 3),
+    ("block", 1, 3), ("small", 3), ("end_back", 1), ("sum", 0, 5), ("sum", 4, 0), ("sum", 0, 4), ("sum", 2, 2),
+    ("sum", 3, 1), ("sum", 1, 5), ("sum", 3, 2), ("sum", 1, 4), ("sum", 4, 3), ("sum", 2, 5), ("pass", 0, 1, 1),
+    ("sum", 5, 0), ("sum", 4, 1), ("sum", 4, 2), ("sum", 2, 4), ("sum", 5, 3), ("sum", 3, 5), ("sum", 6, 0),
+    ("sum", 5, 1), ("sum", 3, 4), ("send", 1, 0), ("sum", 5, 2), ("sum", 7, 0), ("sum", 6, 3), ("sum", 6, 2),
+    ("sum", 4, 5), ("sum", 6, 1), ("sum", 4, 4), ("pass", 1, 0, 0), ("sum", 5, 5), ("send", 1, 1), ("sum", 7, 3),
+    ("sum", 7, 2), ("send", 1, 2), ("sum", 5, 4), ("sum", 7, 1), ("sum", 6, 5), ("sum", 6, 4), ("pass", 1, 1, 0),
+    ("pass", 1, 0, 1), ("sum", 8, 2), ("sum", 8, 1), ("pass", 0, 0, 2), ("sum", 7, 5), ("sum", 8, 0), ("sum", 7, 4),
+    ("sum", 8, 5), ("pass", 1, 0, 2), ("sum", 8, 3), ("sum", 8, 4), ("pass", 1, 1, 1), ("pass", 1, 2, 0),
 )
 
 
@@ -228,7 +228,7 @@
         b_in_hbm, b_back_hbm, tokens_hbm, cot_hbm, wq_hbm, wk_hbm, wv_hbm, wo_hbm, w_in_hbm, w_back_hbm,
         outputs, grad_input, total, small_out,
         b_in, b_back, cot, wq, wk, wv, wo, w_in, w_back, load_sem,
-        x_all, x_t, k_all, v_all, k_t, v_t, q_m, do_m, score, prob_bf, grad_bf, top, norm, o_t, attn_t, do_t,
+        x_all, x_t, k_all, v_all, k_t, v_t, q_m, do_m, score, bias, prob_bf, grad_bf, top, norm, o_t, attn_t, do_t,
         live_branch, resid, resid_bf, resid_t, grad_ffn, ffn, grad_x, lse, delta,
         dq_t, dk, dv, acc, back_in,
         x_send, x_recv, r_send, r_recv,
@@ -260,8 +260,7 @@
         src, dst = pairs_of[i - seqs]
         return pltpu.make_async_copy(src, dst, load_sem.at[i])
 
-    for i in range(seqs + 9):
-        load(i).start()
+    load(0).start()
 
     def x_copy(s, j, h):
         here = pl.ds(h * (rows // 2), rows // 2)
@@ -283,6 +282,8 @@
     peers = [plan.partner(axis, bit) for axis, bit in plane] + [(b, (z + d) % n) for d in range(1, n)]
     for peer in peers:
         pl.semaphore_signal(barrier, inc=1, device_id=peer, device_id_type=MESH)
+    for i in range(1, seqs + 9):
+        load(i).start()
     pl.semaphore_wait(barrier, len(peers))
 
     def send_own(s):
@@ -291,10 +292,10 @@
             for h in (0, 1):
                 x_copy(s, z, h).start()
 
-    for s in range(seqs):
+    load(0).wait()
+    send_own(0)
+    for s in range(1, seqs):
         load(s).wait()
-        if s == 0:
-            send_own(0)
 
     for i in range(3):
         load(seqs + i).wait()
@@ -322,19 +323,19 @@
         k_all[front], v_all[here] = keys, values
         k_t[here], v_t[front] = keys.T, values.T
 
-    def allowed(s, j):
+    def forbid(s, j):
         limit = jnp.minimum(query_pos + 1, lens[s]) - j * rows
-        return key_iota < limit
-
-    def scores_of(s, j, head, mask):
+        bias[...] = jnp.where(key_iota < limit, 0.0, NEG)
+
+    def scores_of(s, j, head):
         p, half = head // 2, slice(head % 2 * rows, (head % 2 + 1) * rows)
         keys = k_all[forward_slot(s, j), :, p * PAIR : (p + 1) * PAIR]
-        return jnp.where(mask, mm_nt(keys, q_m[s, p, half]), NEG)
+        return mm_nt(keys, q_m[s, p, half]) + bias[...]
 
     def statistics(s, j):
-        mask = allowed(s, j)
+        forbid(s, j)
         for head in range(HEADS):
-            score[head] = scores_of(s, j, head, mask)
+            score[head] = scores_of(s, j, head)
         for head in range(HEADS):
             old = top[s, head]
             new = jnp.maximum(old, jnp.max(score[head], axis=0, keepdims=True))
@@ -343,10 +344,10 @@
             top[s, head] = new
 
     def probabilities(s, j):
-        mask = allowed(s, j)
+        forbid(s, j)
         for head in range(HEADS):
             p, half = head // 2, slice(head % 2 * rows, (head % 2 + 1) * rows)
-            probs = jnp.exp(scores_of(s, j, head, mask) - lse[s, head])
+            probs = jnp.exp(scores_of(s, j, head) - lse[s, head])
             prob_bf[slot(s, j), p, :, half] = probs.astype(BF)
 
     def mix_values(s, j):
@@ -782,6 +783,7 @@
             pltpu.VMEM((seqs, HEADS // 2, 2 * rows, PAIR), BF),
             pltpu.VMEM((HEADS // 2, 2 * rows, PAIR), BF),
             pltpu.VMEM((HEADS, rows, rows), F32),
+            pltpu.VMEM((rows, rows), F32),
             pltpu.VMEM((slots, HEADS // 2, rows, 2 * rows), BF),
             pltpu.VMEM((HEADS // 2, rows, 2 * rows), BF),
             pltpu.VMEM((seqs, HEADS, 1, rows), F32),

time: 120 us -> 118 us (0.983)
  Pallas kernels: 118 us -> 116 us
    pallas_call x1, Pallas kernels: 112 us -> 110 us  [per_device(): pl.pallas_call(functools.partial(layer_kernel, plan, n, keep), out_shape=...]
where the time goes in v3:
time: 118 us
  Pallas kernels  116 us (98%)
  between operations  2.11 us (2%)
    pallas_call x1, Pallas kernels, per_device(): pl.pallas_call(functools.partial(layer_kernel, plan, n, keep), out_shape=...  110 us
    pallas_call x1, Pallas kernels, expand(): pl.pallas_call(functools.partial(expand_kernel, cols), out_shape=(jax.Sha...  5.67 us

profile of v3, /device:TPU:0, one launch (start us, length us, event | category | flops | bytes accessed | tf_op | source)
XLA Modules:
  0.0 118.0 jit_solution(15065514827215310892)
XLA Ops:
  1.9 110.2 %layer.1 = (bf16[2,256,512]{2,1,0:T(8,128)(2,1)S(1)}, bf16[2,256,512]{2,1,0:T(8,128)(2,1)S(1)}, bf16[6,1024,512]{2,1,0:T(8,128)(2,1)S(1)}, f32[8,512]{1,0:T(8,128)S(1)}) custom-call(s32[2]{0:T(128)} %lens.1, f32[1]{0:T(128)} %bitcast.8.alpha_attn_ref, f32[1]{0:T(128)} %bitcast.9.alpha_ffn_ref, f32[1,2048]{1,0:T(1,128)} %bitcast.10, f32[1,512]{1,0:T(1,128)} %bitcast.11, ...), custom_call_target="tpu_custom_call" | custom-call | tf_op jit(solution)/shard_map/layer/pallas_call | solution.py:760
  112.1 5.7 %expand.1 = (f32[2048,512]{1,0:T(8,128)}, f32[512,2048]{1,0:T(8,128)}, f32[512,512]{1,0:T(8,128)}, f32[512,512]{1,0:T(8,128)}, f32[512,512]{1,0:T(8,128)}, /*ind...) custom-call(bf16[6,1024,512]{2,1,0:T(8,128)(2,1)S(1)} %get-tuple-ele, ...), custom_call_target="tpu_custom_call" | custom-call | tf_op jit(solution)/shard_map/expand/pallas_call | solution.py:717
